TPU v7x, 32 devices: a whole 2x2x4 slice. The times are simulated.
32 devices in a mesh: groups: 2 (over x), pairs: 16 (over z, y, core), win: 1.
Axes of the slice: x: 2, y: 2, z: 4, core: 2. Of those that a mesh axis runs over, the one named last changes fastest.
Arguments:
- traces: bfloat16 [512, 3, 2, 2048], P(('groups', 'pairs'), None, 'win'), parts along dimension 0, may hold values from -6 to 6
- valid: int32 [512, 2], P(('groups', 'pairs'), 'win'), parts along dimension 0, may hold values 0 or 1
- pair_list: int32 [512, 2], P('groups'), parts along dimension 0, may hold values from 0 to 127, as said below
Outputs:
- stacks: float32 [512, 36, 2048], P(('groups', 'pairs', 'win')), parts along dimension 0
There are 2 independent parts, one for each index of `groups`. A program takes and returns all parts, laid end to end along the dimension named above; each array names one. Nothing has to cross between parts.
Inputs may be any that keep to these rules, and one draw needn't show every extreme that they name: `pair_list`: row r belongs to owner r // 16, and block b to index b // 8 of pairs. The 32 entries of each owner name distinct blocks on exactly 8 indices of pairs, 4 on each.
All inputs are finite; a program needn't handle non-finite values. No bound on the sum of `valid` on one device may be relied on, other than what follows from the above.
Results may differ from a plain program's by a relative error of at most 0.0052.
Values may be sent and summed in bfloat16 or wider, within the bound.
A program may use at most 128 MiB of HBM per device.

v0:
```python
import functools
import math

import jax
import jax.numpy as jnp
import ml_dtypes
import numpy as np
from jax import lax
from jax.experimental import pallas as pl
from jax.experimental.pallas import tpu as pltpu
from jax.sharding import PartitionSpec as P

BAND = 64
SB = 2
ROWS = SB * 3
CORRS = ROWS * ROWS
PAD = 40
TILE = 256


def tables(samples):
    period = 2 * samples
    angle = np.arange(period, dtype=np.float32) * np.float32(2.0 * math.pi / period)
    cosine, sine = np.cos(angle), np.sin(angle)
    index = np.arange(samples, dtype=np.int32)
    forward = index[:, None] * index[None, :] % period
    inverse = index[:, None] * (index[None, :] - samples // 2) % period
    weight = np.where(index[:, None] == 0, 1.0, 2.0).astype(np.float32) / np.float32(math.sqrt(period))
    first = np.stack([cosine[forward], -sine[forward]]).astype(ml_dtypes.bfloat16)
    second = np.stack([weight * cosine[inverse], -weight * sine[inverse]]).astype(ml_dtypes.bfloat16)
    return first, second


def stack_kernel(pairs, windows, x_ref, fwd_ref, band_ref, inv_ref, out_ref, white, cross, total):
    step = pl.program_id(0)
    steps = pl.num_programs(0)
    x = x_ref[...]
    real = jnp.dot(x, fwd_ref[0], preferred_element_type=jnp.float32)
    imag = jnp.dot(x, fwd_ref[1], preferred_element_type=jnp.float32)
    magnitude = jnp.sqrt(real * real + imag * imag)
    high = magnitude.astype(jnp.bfloat16)
    low = (magnitude - high.astype(jnp.float32)).astype(jnp.bfloat16)
    band = jnp.dot(high, band_ref[...], preferred_element_type=jnp.float32) + jnp.dot(
        low, band_ref[...], preferred_element_type=jnp.float32
    )
    scale = 1.0 / (band + 1e-06)
    white[0] = (real * scale).astype(jnp.bfloat16).astype(jnp.float32)
    white[1] = (imag * scale).astype(jnp.bfloat16).astype(jnp.float32)
    for lane in range(0, TILE, 128):
        lanes = slice(lane, lane + 128)
        for p0 in range(0, pairs, 8):

            def value(side, i, w, part):
                row = ((side * ROWS + i) * windows + w) * pairs + p0
                return white[part, row : row + 8, lanes]

            for i in range(ROWS):
                mine = [(value(0, i, w, 0), value(0, i, w, 1)) for w in range(windows)]
                for j in range(ROWS):
                    re = im = None
                    for w in range(windows):
                        ar, ai = mine[w]
                        br, bi = value(1, j, w, 0), value(1, j, w, 1)
                        re_w = ar * br + ai * bi
                        im_w = ar * bi - ai * br
                        re = re_w if re is None else re + re_w
                        im = im_w if im is None else im + im_w
                    spot = pl.ds(p0 * PAD + i * ROWS + j, 8, stride=PAD)
                    k = lane // 128
                    cross[0, k, spot, :] = re * (1.0 / windows)
                    cross[1, k, spot, :] = im * (1.0 / windows)
    count = TILE // 128
    both = jnp.concatenate(
        [cross[part, k].astype(jnp.bfloat16) for part in range(2) for k in range(count)], axis=1
    )
    samples = out_ref.shape[-1]
    wide = 512

    def lags(at):
        table = jnp.concatenate([inv_ref[0, :, at], inv_ref[1, :, at]], axis=0)
        return jnp.dot(both, table, preferred_element_type=jnp.float32)

    @pl.when(step == 0)
    def _():
        for t in range(0, samples, wide):
            total[:, t : t + wide] = lags(slice(t, t + wide))

    @pl.when((step > 0) & (step < steps - 1))
    def _():
        for t in range(0, samples, wide):
            total[:, t : t + wide] += lags(slice(t, t + wide))

    @pl.when(step == steps - 1)
    def _():
        for t in range(0, samples, wide):
            done = total[:, t : t + wide] + lags(slice(t, t + wide))
            for p in range(pairs):
                out_ref[p, :, t : t + wide] = done[p * PAD : p * PAD + CORRS]


def stack(x, pairs, windows):
    samples = x.shape[-1]
    first, second = tables(samples)
    runs = np.arange(TILE) // BAND
    band = ((runs[:, None] == runs[None, :]) / BAND).astype(ml_dtypes.bfloat16)
    return pl.pallas_call(
        functools.partial(stack_kernel, pairs, windows),
        out_shape=jax.ShapeDtypeStruct((pairs, CORRS, samples), jnp.float32),
        grid=(samples // TILE,),
        in_specs=[
            pl.BlockSpec(x.shape, lambda j: (0, 0)),
            pl.BlockSpec((2, samples, TILE), lambda j: (0, 0, j)),
            pl.BlockSpec((TILE, TILE), lambda j: (0, 0)),
            pl.BlockSpec((2, TILE, samples), lambda j: (0, j, 0)),
        ],
        out_specs=pl.BlockSpec((pairs, CORRS, samples), lambda j: (0, 0, 0)),
        scratch_shapes=[
            pltpu.VMEM((2, x.shape[0], TILE), jnp.float32),
            pltpu.VMEM((2, TILE // 128, pairs * PAD, 128), jnp.float32),
            pltpu.VMEM((pairs * PAD, samples), jnp.float32),
        ],
        compiler_params=pltpu.CompilerParams(vmem_limit_bytes=56 * 2**20),
        cost_estimate=pl.CostEstimate(
            flops=4 * (x.shape[0] + pairs * PAD) * samples * samples,
            bytes_accessed=8 * samples * samples + 4 * pairs * CORRS * samples,
            transcendentals=x.shape[0] * samples,
        ),
        name="stack",
    )(x, jnp.asarray(first), jnp.asarray(band), jnp.asarray(second))


def local(traces, valid, pair_list):
    owners = lax.axis_size("pairs")
    window_devs = lax.axis_size("win")
    samples = traces.shape[-1]
    per_window = traces.shape[2]
    windows = per_window * window_devs
    blk_count = traces.shape[0] // SB
    pairs = pair_list.shape[0] // (owners * window_devs)
    own_rows = blk_count * ROWS * per_window
    masked = traces * valid[:, None, :, None].astype(traces.dtype)
    everything = lax.all_gather(
        masked.reshape(own_rows, samples), ("pairs", "win"), axis=0, tiled=True
    )
    place = lax.axis_index("pairs") * window_devs + lax.axis_index("win")
    mine = lax.dynamic_slice_in_dim(pair_list, place * pairs, pairs, 0).T
    blocks = mine[:, None, None, None, :]
    i = jnp.arange(ROWS)[None, :, None, None, None]
    v = jnp.arange(window_devs)[None, None, :, None, None]
    w = jnp.arange(per_window)[None, None, None, :, None]
    device = blocks // blk_count * window_devs + v
    wanted = device * own_rows + ((blocks % blk_count) * ROWS + i) * per_window + w
    chosen = wanted.reshape(-1, 1) == jnp.arange(everything.shape[0])[None, :]
    x = jnp.dot(chosen.astype(jnp.bfloat16), everything, preferred_element_type=jnp.bfloat16)
    return stack(x, pairs, windows)


def solution(mesh):
    in_specs = (
        P(("groups", "pairs"), None, "win", None),
        P(("groups", "pairs"), "win"),
        P("groups", None),
    )
    out_specs = P(("groups", "pairs", "win"), None, None)
    return jax.shard_map(local, mesh=mesh, in_specs=in_specs, out_specs=out_specs, check_vma=False)
```

profile of v0, /device:TPU:13, one launch (start us, length us, event | category | flops | bytes accessed | tf_op | source)
XLA Modules:
  0.0 124.9 jit_solution(11988718383151853605)
XLA Ops:
  6.5 0.0 all-gather.2.cloned.1.call-start
  6.5 0.7 convert_element_type.5
  7.2 0.1 copy.7
  7.3 1.4 %broadcast_multiply_fusion = bf16[16,3,2,2048]{3,2,1,0:T(2,128)(2,1)S(1)} fusion(bf16[16,3,2,2048]{3,2,1,0:T(2,128)(2,1)} %param.6, bf16[16,2]{1,0:T(8,128)(2,1)S(1)} %copy.7), kind=kLoop, calls=%fused_computation.3 | loop fusion | flops 196608 | bytes 786496 | tf_op jit(solution)/shard_map/mul | solution.py:141
  8.7 0.9 reshape.65
  9.6 0.0 all-gather.2.cloned.1.call-update
  9.7 0.8 fusion.3
  10.4 0.1 add.76
  10.5 61.7 %all-gather.2.cloned.1.call-done = bf16[1536,2048]{1,0:T(8,128)(2,1)} async-done(((bf16[96,2048]{1,0:T(8,128)(2,1)}), bf16[1536,2048]{1,0:T(8,128)(2,1)}) %all-gather.2.cloned.1.call-update) | async-done | bytes 6291472 | tf_op jit(solution)/shard_map/all_gather | solution.py:142
  72.3 6.6 %fusion.x_ref = bf16[384,2048]{1,0:T(8,128)(2,1)} fusion(bf16[1536,2048]{1,0:T(8,128)(2,1)} %all-gather.2.cloned.1.call-done, s32[384]{0:T(512)S(1)} %add.76), kind=kOutput, calls=%fused_computation.1 | convolution fusion | flops 2416508928 | bytes 7865856 | tf_op jit(solution)/shard_map/dot_general | solution.py:154
  78.8 31.9 %stack.1 = f32[16,36,2048]{2,1,0:T(8,128)} custom-call(bf16[384,2048]{1,0:T(8,128)(2,1)} %fusion.x_ref, bf16[2,2048,2048]{2,1,0:T(8,128)(2,1)} %constant.51.clone.fwd_ref, bf16[256,256]{1,0:T(8,128)(2,1)} %constant.52.clone.band_ref, bf16[2,2048,2048]{2,1,0:T(8,128)(2,1)} %constant.53.clone.inv_ref), custom_call_target="tpu_custom_call" | custom-call | flops 17179869184 | bytes 38273024 | tf_op jit(solution)/shard_map/stack/pallas_call | solution.py:106
  110.7 7.4 %copy.8 = f32[16,36,2048]{2,0,1:T(8,128)} copy(f32[16,36,2048]{2,1,0:T(8,128)} %stack.1) | data formatting | bytes 9437184 | tf_op jit(solution)/shard_map/stack/pallas_call | solution.py:106
  (2 shorter events, 0.0 us)
Async XLA Ops:
  6.5 65.7 %all-gather.2.cloned.1.call-start = ((), (), s32[]{:S(2)}) async-start(), calls=%async_computation | async-start | bytes 6684672 | tf_op jit(solution)/shard_map/all_gather | solution.py:142
Sparse Core Ops, SparseCore 0:
  9.8 62.4 all-gather.1
where the time goes:
time: 127 us; the launch traced here: 125 us
  waiting for transfers between devices  61.7 us (49%)
  Pallas kernels  31.9 us (25%)
  between operations  13.4 us (11%)
  local copies, waits for them, and re-layouts  8.49 us (7%)
  matrix products  6.55 us (5%)
  other arithmetic  2.88 us (2%)
    all_gather x1, waiting for transfers between devices, local(): lax.all_gather(masked.reshape(own_rows, samples), ('pairs', 'win'), axis=...  61.7 us
    pallas_call x1, Pallas kernels, stack(): pl.pallas_call(functools.partial(stack_kernel, pairs, windows), out_shape...  31.9 us
    pallas_call x1, local copies, waits for them, and re-layouts, stack(): pl.pallas_call(functools.partial(stack_kernel, pairs, windows), out_shape...  7.4 us
    dot_general x1, matrix products, local(): jnp.dot(chosen.astype(jnp.bfloat16), everything, preferred_element_type=j...  6.55 us
  transfers between devices with their start and end apart: 1, of which 1 were waited for; matrix products, arithmetic and copies ran while one was open for 1% of the time, Pallas kernels for 0%

commit v1 on v0

v1 whole, which is shorter than its diff:
```python
import functools
import math

import jax
import jax.numpy as jnp
import ml_dtypes
import numpy as np
from jax import lax
from jax.experimental import pallas as pl
from jax.experimental.pallas import tpu as pltpu
from jax.sharding import PartitionSpec as P

BAND = 64
SB = 2
ROWS = SB * 3
CORRS = ROWS * ROWS
TILE = 256


def tables(samples):
    period = 2 * samples
    angle = np.arange(period, dtype=np.float32) * np.float32(2.0 * math.pi / period)
    cosine, sine = np.cos(angle), np.sin(angle)
    index = np.arange(samples, dtype=np.int32)
    forward = index[:, None] * index[None, :] % period
    inverse = index[:, None] * (index[None, :] - samples // 2) % period
    weight = np.where(index[:, None] == 0, 1.0, 2.0).astype(np.float32) / np.float32(math.sqrt(period))
    first = np.stack([cosine[forward], -sine[forward]]).astype(ml_dtypes.bfloat16)
    second = np.stack([weight * cosine[inverse], -weight * sine[inverse]]).astype(ml_dtypes.bfloat16)
    return first, second


def stack_kernel(pairs, windows, x_ref, fwd_ref, band_ref, inv_ref, out_ref, white, cross):
    @pl.when(pl.program_id(0) == 0)
    def _():
        out_ref[...] = jnp.zeros_like(out_ref)

    x = x_ref[...]
    real = jnp.dot(x, fwd_ref[0], preferred_element_type=jnp.float32)
    imag = jnp.dot(x, fwd_ref[1], preferred_element_type=jnp.float32)
    magnitude = jnp.sqrt(real * real + imag * imag)
    high = magnitude.astype(jnp.bfloat16)
    low = (magnitude - high.astype(jnp.float32)).astype(jnp.bfloat16)
    band = jnp.dot(high, band_ref[...], preferred_element_type=jnp.float32) + jnp.dot(
        low, band_ref[...], preferred_element_type=jnp.float32
    )
    scale = 1.0 / (band + 1e-06)
    white[0] = (real * scale).astype(jnp.bfloat16).astype(jnp.float32)
    white[1] = (imag * scale).astype(jnp.bfloat16).astype(jnp.float32)
    for lane in range(0, TILE, 128):
        lanes = slice(lane, lane + 128)
        for p0 in range(0, pairs, 8):

            def value(side, i, w, part):
                row = ((side * ROWS + i) * windows + w) * pairs + p0
                return white[part, row : row + 8, lanes]

            for i in range(ROWS):
                mine = [(value(0, i, w, 0), value(0, i, w, 1)) for w in range(windows)]
                for j in range(ROWS):
                    re = im = None
                    for w in range(windows):
                        ar, ai = mine[w]
                        br, bi = value(1, j, w, 0), value(1, j, w, 1)
                        re_w = ar * br + ai * bi
                        im_w = ar * bi - ai * br
                        re = re_w if re is None else re + re_w
                        im = im_w if im is None else im + im_w
                    row = (i * ROWS + j) * pairs + p0
                    cross[row : row + 8, lanes] = re * (1.0 / windows)
                    cross[row : row + 8, TILE + lane : TILE + lane + 128] = im * (1.0 / windows)
    both = cross[...].astype(jnp.bfloat16)
    samples = out_ref.shape[-1]
    wide = 512
    for t in range(0, samples, wide):
        table = jnp.concatenate([inv_ref[0, :, t : t + wide], inv_ref[1, :, t : t + wide]], axis=0)
        out_ref[:, t : t + wide] += jnp.dot(both, table, preferred_element_type=jnp.float32)


def stack(x, pairs, windows):
    samples = x.shape[-1]
    first, second = tables(samples)
    runs = np.arange(TILE) // BAND
    band = ((runs[:, None] == runs[None, :]) / BAND).astype(ml_dtypes.bfloat16)
    out = pl.pallas_call(
        functools.partial(stack_kernel, pairs, windows),
        out_shape=jax.ShapeDtypeStruct((CORRS * pairs, samples), jnp.float32),
        grid=(samples // TILE,),
        in_specs=[
            pl.BlockSpec(x.shape, lambda j: (0, 0)),
            pl.BlockSpec((2, samples, TILE), lambda j: (0, 0, j)),
            pl.BlockSpec((TILE, TILE), lambda j: (0, 0)),
            pl.BlockSpec((2, TILE, samples), lambda j: (0, j, 0)),
        ],
        out_specs=pl.BlockSpec((CORRS * pairs, samples), lambda j: (0, 0)),
        scratch_shapes=[
            pltpu.VMEM((2, x.shape[0], TILE), jnp.float32),
            pltpu.VMEM((CORRS * pairs, 2 * TILE), jnp.float32),
        ],
        compiler_params=pltpu.CompilerParams(vmem_limit_bytes=56 * 2**20),
        cost_estimate=pl.CostEstimate(
            flops=4 * (x.shape[0] + pairs * CORRS) * samples * samples,
            bytes_accessed=8 * samples * samples + 4 * pairs * CORRS * samples,
            transcendentals=x.shape[0] * samples,
        ),
        name="stack",
    )(x, jnp.asarray(first), jnp.asarray(band), jnp.asarray(second))
    return out.reshape(CORRS, pairs, samples).transpose(1, 0, 2)


def local(traces, valid, pair_list):
    owners = lax.axis_size("pairs")
    window_devs = lax.axis_size("win")
    me = lax.axis_index("pairs")
    samples = traces.shape[-1]
    per_window = traces.shape[2]
    windows = per_window * window_devs
    blk_count = traces.shape[0] // SB
    pair_count = pair_list.shape[0] // owners
    pairs = pair_count // window_devs
    capacity = max(1, 4 * pair_count // owners)
    series = ROWS * per_window
    masked = (traces * valid[:, None, :, None].astype(traces.dtype)).reshape(-1, samples)

    requests = pair_list.reshape(owners, 2 * pair_count)
    sources = requests // blk_count
    ids = jnp.arange(2 * pair_count, dtype=jnp.int32)
    earlier = ids[None, :] < ids[:, None]
    ranks = jnp.sum((sources[:, :, None] == sources[:, None, :]) & earlier[None], axis=-1)
    slots = jnp.arange(capacity, dtype=jnp.int32)
    found = (sources == me)[:, None, :] & (ranks[:, None, :] == slots[None, :, None])
    picked = jnp.sum(jnp.where(found, requests[:, None, :] % blk_count + 1, 0), axis=-1) - 1
    picked = jnp.broadcast_to(picked[:, None], (owners, window_devs, capacity)).reshape(-1, 1)
    serial = jnp.arange(series, dtype=jnp.int32)
    from_rows = jnp.where(picked < 0, -1, picked * series + serial).reshape(-1, 1)
    sending = from_rows == jnp.arange(masked.shape[0], dtype=jnp.int32)[None, :]
    sent = jnp.dot(sending.astype(jnp.bfloat16), masked, preferred_element_type=jnp.bfloat16)
    received = lax.all_to_all(
        sent.reshape(owners * window_devs, capacity * series, samples),
        ("pairs", "win"),
        split_axis=0,
        concat_axis=0,
        tiled=True,
    ).reshape(-1, samples)

    def kept(array):
        own = lax.dynamic_index_in_dim(array, me, 0, keepdims=False).reshape(pair_count, 2)
        own = lax.dynamic_slice_in_dim(own, lax.axis_index("win") * pairs, pairs, 0)
        return own.T[:, None, None, None, :]

    i = jnp.arange(ROWS, dtype=jnp.int32)[None, :, None, None, None]
    v = jnp.arange(window_devs, dtype=jnp.int32)[None, None, :, None, None]
    w = jnp.arange(per_window, dtype=jnp.int32)[None, None, None, :, None]
    slot = (kept(sources) * window_devs + v) * capacity + kept(ranks)
    wanted = (slot * ROWS + i) * per_window + w
    chosen = wanted.reshape(-1, 1) == jnp.arange(received.shape[0], dtype=jnp.int32)[None, :]
    x = jnp.dot(chosen.astype(jnp.bfloat16), received, preferred_element_type=jnp.bfloat16)
    return stack(x, pairs, windows)


def solution(mesh):
    in_specs = (
        P(("groups", "pairs"), None, "win", None),
        P(("groups", "pairs"), "win"),
        P("groups", None),
    )
    out_specs = P(("groups", "pairs", "win"), None, None)
    return jax.shard_map(local, mesh=mesh, in_specs=in_specs, out_specs=out_specs, check_vma=False)
```

time: 127 us -> 115 us (0.906); the launches traced: 125 us -> 114 us
  between operations: 13.4 us -> 0.08 us
  waiting for transfers between devices: 61.7 us -> 69.6 us
  starting transfers between devices: 0.01 us -> 6.55 us
  local copies, waits for them, and re-layouts: 8.49 us -> 2.02 us
  Pallas kernels: 31.9 us -> 28 us
    all_to_all x0 -> x1, waiting for transfers between devices: none -> 69.6 us  [local(): lax.all_to_all(sent.reshape(owners * window_devs, capacity * series, samp...]
    all_gather x1 -> x0, waiting for transfers between devices: 61.7 us -> none  [local(): lax.all_gather(masked.reshape(own_rows, samples), ('pairs', 'win'), axis=...]
    pallas_call x1 -> x0, local copies, waits for them, and re-layouts: 7.4 us -> none  [stack(): pl.pallas_call(functools.partial(stack_kernel, pairs, windows), out_shape...]
    all_to_all x0 -> x1, starting transfers between devices: none -> 6.55 us  [local(): lax.all_to_all(sent.reshape(owners * window_devs, capacity * series, samp...]
    pallas_call x1, Pallas kernels: 31.9 us -> 28 us  [stack(): pl.pallas_call(functools.partial(stack_kernel, pairs, windows), out_shape...]
    dot_general x1 -> x2, matrix products: 6.55 us -> 5.28 us  [the longest x1 2.69 us: local(): jnp.dot(sending.astype(jnp.bfloat16), masked, preferred_element_type=jnp....]
  transfers between devices with their start and end apart: 1 -> 1, of which waited for: 1 -> 1; matrix products, arithmetic and copies ran while one was open for 1% -> 0% of each run, Pallas kernels for 0% -> 0%
where the time goes in v1:
time: 115 us; the launch traced here: 114 us
  waiting for transfers between devices  69.6 us (61%)
  Pallas kernels  28 us (24%)
  starting transfers between devices  6.55 us (6%)
  matrix products  5.28 us (5%)
  other arithmetic  2.81 us (2%)
  local copies, waits for them, and re-layouts  2.02 us (2%)
    all_to_all x1, waiting for transfers between devices, local(): lax.all_to_all(sent.reshape(owners * window_devs, capacity * series, samp...  69.6 us
    pallas_call x1, Pallas kernels, stack(): pl.pallas_call(functools.partial(stack_kernel, pairs, windows), out_shape...  28 us
    all_to_all x1, starting transfers between devices, local(): lax.all_to_all(sent.reshape(owners * window_devs, capacity * series, samp...  6.55 us
    dot_general x1, matrix products, local(): jnp.dot(sending.astype(jnp.bfloat16), masked, preferred_element_type=jnp....  2.69 us
    dot_general x1, matrix products, local(): jnp.dot(chosen.astype(jnp.bfloat16), received, preferred_element_type=jnp...  2.59 us
  transfers between devices with their start and end apart: 1, of which 1 were waited for; matrix products, arithmetic and copies ran while one was open for 0% of the time, Pallas kernels for 0%

profile of v1, /device:TPU:13, one launch (start us, length us, event | category | flops | bytes accessed | tf_op | source)
XLA Modules:
  0.0 114.3 jit_solution(3580481941688062471)
XLA Ops:
  0.0 0.8 copy.12
  0.8 0.1 reshape.229
  1.0 0.5 convert_reduce_fusion
  1.4 0.2 select_reduce_fusion
  1.6 0.7 convert_element_type.10
  2.3 0.1 copy.16
  2.4 0.1 add.132
  2.5 0.1 copy.14
  2.6 0.1 broadcast_in_dim.28
  2.7 0.1 broadcast_in_dim.29
  2.8 0.1 copy.15
  2.8 0.1 add.129
  2.9 0.1 add.130
  3.0 1.4 %broadcast_multiply_fusion = bf16[16,3,2,2048]{3,2,1,0:T(2,128)(2,1)S(1)} fusion(bf16[16,3,2,2048]{3,2,1,0:T(2,128)(2,1)} %param.6, bf16[16,2]{1,0:T(8,128)(2,1)S(1)} %copy.16), kind=kLoop, calls=%fused_computation.7 | loop fusion | flops 196608 | bytes 786496 | tf_op jit(solution)/shard_map/mul | solution.py:123
  4.4 0.1 reshape.233
  4.6 2.7 %fusion.3 = bf16[16,48,2048]{2,1,0:T(8,128)(2,1)} fusion(bf16[96,2048,1]{1,0,2:T(8,128)(2,1)S(1)} %reshape.233, s32[16,48]{1,0:T(8,128)S(1)} %add_select_fusion.2), kind=kOutput, calls=%fused_computation.5 | convolution fusion | flops 302063616 | bytes 3542016 | tf_op jit(solution)/shard_map/dot_general | solution.py:137
  7.3 6.6 %all-to-all-start = ((bf16[16,48,2048]{2,1,0:T(8,128)(2,1)}), bf16[16,48,2048]{2,1,0:T(8,128)(2,1)S(1)}, u32[]{:S(2)}, u32[]{:S(2)}) async-start(bf16[16,48,2048]{2,1,0:T(8,128)(2,1)} %fusion.3), calls=%async_computation | async-start | bytes 6291456 | tf_op jit(solution)/shard_map/all_to_all | solution.py:138
  13.9 0.1 mul.59
  14.0 0.1 copy.13
  14.1 0.1 add.126
  14.2 69.6 %all-to-all-done = bf16[16,48,2048]{2,1,0:T(8,128)(2,1)S(1)} async-done(((bf16[16,48,2048]{2,1,0:T(8,128)(2,1)}), bf16[16,48,2048]{2,1,0:T(8,128)(2,1)S(1)}, u32[]{:S(2)}, u32[]{:S(2)}) %all-to-all-start) | async-done | bytes 3145760 | tf_op jit(solution)/shard_map/all_to_all | solution.py:138
  83.7 2.6 %fusion.x_ref = bf16[384,2048]{1,0:T(8,128)(2,1)} fusion(bf16[768,2048]{1,0:T(8,128)(2,1)S(1)} %bitcast.10, s32[384]{0:T(512)S(1)} %add.126), kind=kOutput, calls=%fused_computation.1 | convolution fusion | flops 1208254464 | bytes 4720128 | tf_op jit(solution)/shard_map/dot_general | solution.py:157
  86.3 28.0 %stack.1 = f32[576,2048]{1,0:T(8,128)} custom-call(bf16[384,2048]{1,0:T(8,128)(2,1)} %fusion.x_ref, bf16[2,2048,2048]{2,1,0:T(8,128)(2,1)} %constant.61.clone.fwd_ref, bf16[256,256]{1,0:T(8,128)(2,1)} %constant.62.clone.band_ref, bf16[2,2048,2048]{2,1,0:T(8,128)(2,1)} %constant.63.clone.inv_ref), custom_call_target="tpu_custom_call" | custom-call | flops 16106127360 | bytes 38273024 | tf_op jit(solution)/shard_map/stack/pallas_call | solution.py:85
  (10 shorter events, 0.1 us)
Async XLA Ops:
  7.3 76.4 %all-to-all-start = ((bf16[16,48,2048]{2,1,0:T(8,128)(2,1)}), bf16[16,48,2048]{2,1,0:T(8,128)(2,1)S(1)}, u32[]{:S(2)}, u32[]{:S(2)}) async-start(bf16[16,48,2048]{2,1,0:T(8,128)(2,1)} %fusion.3), calls=%async_computation | async-start | bytes 6291456 | tf_op jit(solution)/shard_map/all_to_all | solution.py:138

commit v2 on v1

--- a/solution.py
+++ b/solution.py
@@ -108,6 +108,69 @@
     return out.reshape(CORRS, pairs, samples).transpose(1, 0, 2)
 
 
+def exchange_kernel(count, window_devs, sent_ref, got_ref, send_sem, recv_sem, own_sem):
+    me = lax.axis_index("pairs") * window_devs + lax.axis_index("win")
+    group = lax.axis_index("groups")
+
+    def device(index):
+        return (group, index // window_devs, index % window_devs)
+
+    def copy(distance):
+        peer = lax.rem(me + distance, count)
+        return pltpu.make_async_remote_copy(
+            src_ref=sent_ref.at[peer],
+            dst_ref=got_ref.at[me],
+            send_sem=send_sem.at[distance],
+            recv_sem=recv_sem.at[distance],
+            device_id=device(peer),
+            device_id_type=pl.DeviceIdType.MESH,
+        )
+
+    barrier = pltpu.get_barrier_semaphore()
+
+    @pl.loop(1, count)
+    def _(distance):
+        pl.semaphore_signal(
+            barrier,
+            inc=1,
+            device_id=device(lax.rem(me + distance, count)),
+            device_id_type=pl.DeviceIdType.MESH,
+        )
+
+    pl.semaphore_wait(barrier, count - 1)
+
+    @pl.loop(1, count)
+    def _(distance):
+        copy(distance).start()
+
+    own = pltpu.make_async_copy(sent_ref.at[me], got_ref.at[me], own_sem)
+    own.start()
+    own.wait()
+
+    @pl.loop(1, count)
+    def _(distance):
+        copy(distance).wait()
+
+
+def exchange(sent, window_devs):
+    count = sent.shape[0]
+    return pl.pallas_call(
+        functools.partial(exchange_kernel, count, window_devs),
+        out_shape=jax.ShapeDtypeStruct(sent.shape, sent.dtype),
+        in_specs=[pl.BlockSpec(memory_space=pltpu.VMEM)],
+        out_specs=pl.BlockSpec(memory_space=pltpu.VMEM),
+        scratch_shapes=[
+            pltpu.SemaphoreType.DMA((count,)),
+            pltpu.SemaphoreType.DMA((count,)),
+            pltpu.SemaphoreType.DMA,
+        ],
+        compiler_params=pltpu.CompilerParams(
+            collective_id=0, has_side_effects=True, vmem_limit_bytes=40 * 2**20
+        ),
+        name="exchange",
+    )(sent)
+
+
 def local(traces, valid, pair_list):
     owners = lax.axis_size("pairs")
     window_devs = lax.axis_size("win")
@@ -135,12 +198,8 @@
     from_rows = jnp.where(picked < 0, -1, picked * series + serial).reshape(-1, 1)
     sending = from_rows == jnp.arange(masked.shape[0], dtype=jnp.int32)[None, :]
     sent = jnp.dot(sending.astype(jnp.bfloat16), masked, preferred_element_type=jnp.bfloat16)
-    received = lax.all_to_all(
-        sent.reshape(owners * window_devs, capacity * series, samples),
-        ("pairs", "win"),
-        split_axis=0,
-        concat_axis=0,
-        tiled=True,
+    received = exchange(
+        sent.reshape(owners * window_devs, capacity * series, samples), window_devs
     ).reshape(-1, samples)
 
     def kept(array):

time: 115 us -> 110 us (0.957)
  Pallas kernels: 28 us -> 101 us
  waiting for transfers between devices: 69.6 us -> 0 us
  starting transfers between devices: 6.55 us -> 0 us
  matrix products: 5.28 us -> 3.61 us
    pallas_call x0 -> x1, Pallas kernels: none -> 73 us  [exchange(): pl.pallas_call(functools.partial(exchange_kernel, count, window_devs), ou...]
    all_to_all x1 -> x0, waiting for transfers between devices: 69.6 us -> none  [local(): lax.all_to_all(sent.reshape(owners * window_devs, capacity * series, samp...]
    all_to_all x1 -> x0, starting transfers between devices: 6.55 us -> none  [local(): lax.all_to_all(sent.reshape(owners * window_devs, capacity * series, samp...]
    dot_general x1, matrix products: 2.69 us -> 1.02 us  [local(): jnp.dot(sending.astype(jnp.bfloat16), masked, preferred_element_type=jnp....]
  transfers between devices with their start and end apart: 1 -> 0, of which waited for: 1 -> 0; matrix products, arithmetic and copies ran while one was open for 0% -> 0% of each run, Pallas kernels for 0% -> 0%
where the time goes in v2:
time: 110 us; the launch traced here: 109 us
  Pallas kernels  101 us (92%)
  matrix products  3.61 us (3%)
  other arithmetic  2.81 us (3%)
  local copies, waits for them, and re-layouts  2.02 us (2%)
    pallas_call x1, Pallas kernels, exchange(): pl.pallas_call(functools.partial(exchange_kernel, count, window_devs), ou...  73 us
    pallas_call x1, Pallas kernels, stack(): pl.pallas_call(functools.partial(stack_kernel, pairs, windows), out_shape...  28 us
    dot_general x1, matrix products, local(): jnp.dot(chosen.astype(jnp.bfloat16), received, preferred_element_type=jnp...  2.59 us

profile of v2, /device:TPU:13, one launch (start us, length us, event | category | flops | bytes accessed | tf_op | source)
XLA Modules:
  0.0 109.5 jit_solution(16043945343781713481)
XLA Ops:
  0.0 0.7 convert_element_type.10
  0.7 0.1 copy.16
  0.8 0.1 add.132
  0.9 0.8 copy.12
  1.7 0.1 reshape.229
  1.8 0.5 convert_reduce_fusion
  2.3 0.2 select_reduce_fusion
  2.5 0.1 copy.14
  2.6 0.1 broadcast_in_dim.28
  2.7 0.1 broadcast_in_dim.29
  2.8 0.1 copy.15
  2.9 0.1 mul.59
  2.9 0.1 copy.13
  3.1 0.1 add.126
  3.2 0.1 add.129
  3.2 0.1 add.130
  3.3 1.4 %broadcast_multiply_fusion = bf16[16,3,2,2048]{3,2,1,0:T(2,128)(2,1)S(1)} fusion(bf16[16,3,2,2048]{3,2,1,0:T(2,128)(2,1)} %param.6, bf16[16,2]{1,0:T(8,128)(2,1)S(1)} %copy.16), kind=kLoop, calls=%fused_computation.7 | loop fusion | flops 196608 | bytes 786496 | tf_op jit(solution)/shard_map/mul | solution.py:186
  4.7 0.1 reshape.233
  4.9 1.0 fusion.3.sent_ref
  5.9 73.0 %exchange.1 = bf16[16,48,2048]{2,1,0:T(8,128)(2,1)S(1)} custom-call(bf16[16,48,2048]{2,1,0:T(8,128)(2,1)S(1)} %fusion.3.sent_ref), custom_call_target="tpu_custom_call" | custom-call | tf_op jit(solution)/shard_map/exchange/pallas_call | solution.py:157
  78.9 2.6 %fusion.x_ref = bf16[384,2048]{1,0:T(8,128)(2,1)} fusion(bf16[768,2048]{1,0:T(8,128)(2,1)S(1)} %bitcast.10, s32[384]{0:T(512)S(1)} %add.126), kind=kOutput, calls=%fused_computation.1 | convolution fusion | flops 1208254464 | bytes 4720128 | tf_op jit(solution)/shard_map/dot_general | solution.py:216
  81.5 28.0 %stack.1 = f32[576,2048]{1,0:T(8,128)} custom-call(bf16[384,2048]{1,0:T(8,128)(2,1)} %fusion.x_ref, bf16[2,2048,2048]{2,1,0:T(8,128)(2,1)} %constant.61.clone.fwd_ref, bf16[256,256]{1,0:T(8,128)(2,1)} %constant.62.clone.band_ref, bf16[2,2048,2048]{2,1,0:T(8,128)(2,1)} %constant.63.clone.inv_ref), custom_call_target="tpu_custom_call" | custom-call | flops 16106127360 | bytes 38273024 | tf_op jit(solution)/shard_map/stack/pallas_call | solution.py:85
  (10 shorter events, 0.1 us)

commit v3 on v1

--- a/solution.py
+++ b/solution.py
@@ -108,53 +108,143 @@
     return out.reshape(CORRS, pairs, samples).transpose(1, 0, 2)
 
 
+def gather_kernel(shape, own_ref, got_ref, send_sem, recv_sem, own_sem):
+    long, wide, window_devs = shape
+    cores = 2
+    group = lax.axis_index("groups")
+    me = lax.axis_index("pairs") * window_devs + lax.axis_index("win")
+    z, y, c = me // (wide * cores), me // cores % wide, me % cores
+
+    def slot_of(z_, y_, c_):
+        return (z_ * wide + y_) * cores + c_
+
+    ways = (
+        slot_of(z + 1, y, c),
+        slot_of(z - 1, y, c),
+        slot_of(z, wide - 1 - y, c),
+        slot_of(z, y, cores - 1 - c),
+    )
+    RIGHT, LEFT, ACROSS, CORE = range(4)
+
+    def device(index):
+        return (group, index // window_devs, index % window_devs)
+
+    def copy(way, slot, src=None):
+        return pltpu.make_async_remote_copy(
+            src_ref=got_ref.at[slot] if src is None else src,
+            dst_ref=got_ref.at[slot],
+            send_sem=send_sem.at[way, slot],
+            recv_sem=recv_sem.at[slot],
+            device_id=device(ways[way]),
+            device_id_type=pl.DeviceIdType.MESH,
+        )
+
+    def greet(way):
+        pl.semaphore_signal(
+            barrier, inc=1, device_id=device(ways[way]), device_id_type=pl.DeviceIdType.MESH
+        )
+
+    has_right, has_left = z < long - 1, z > 0
+    barrier = pltpu.get_barrier_semaphore()
+    pl.when(has_right)(lambda: greet(RIGHT))
+    pl.when(has_left)(lambda: greet(LEFT))
+    if wide > 1:
+        greet(ACROSS)
+    greet(CORE)
+    ends = jnp.where(has_right, 1, 0) + jnp.where(has_left, 1, 0)
+    pl.semaphore_wait(barrier, ends + (2 if wide > 1 else 1))
+
+    pl.when(has_right)(lambda: copy(RIGHT, me, own_ref).start())
+    pl.when(has_left)(lambda: copy(LEFT, me, own_ref).start())
+    if wide > 1:
+        copy(ACROSS, me, own_ref).start()
+    copy(CORE, me, own_ref).start()
+    own = pltpu.make_async_copy(own_ref, got_ref.at[me], own_sem)
+    own.start()
+
+    def pass_on(slot, way, more):
+        copy(CORE, slot, own_ref).wait_recv()
+        pl.when(more)(lambda: copy(way, slot).start())
+        if wide > 1:
+            copy(ACROSS, slot).start()
+        copy(CORE, slot).start()
+
+    @pl.loop(0, long - 1)
+    def _(s):
+        pl.when(s < z)(lambda: pass_on(slot_of(z - 1 - s, y, c), RIGHT, has_right))
+        pl.when(z + 1 + s < long)(lambda: pass_on(slot_of(z + 1 + s, y, c), LEFT, has_left))
+
+    if wide > 1:
+
+        def pass_across(z_):
+            slot = slot_of(z_, wide - 1 - y, c)
+            copy(CORE, slot, own_ref).wait_recv()
+            copy(CORE, slot).start()
+
+        pass_across(z)
+
+        @pl.loop(0, long - 1)
+        def _(s):
+            pl.when(s < z)(lambda: pass_across(z - 1 - s))
+            pl.when(z + 1 + s < long)(lambda: pass_across(z + 1 + s))
+
+    own.wait()
+
+    @pl.loop(0, long)
+    def _(z_):
+        for y_ in range(wide):
+            copy(CORE, slot_of(z_, y_, cores - 1 - c), own_ref).wait_recv()
+            copy(CORE, slot_of(z_, y_, c)).wait_send()
+        slot = slot_of(z_, y, c)
+        if wide > 1:
+            copy(ACROSS, slot).wait_send()
+        pl.when(has_right & (z_ <= z))(lambda: copy(RIGHT, slot).wait_send())
+        pl.when(has_left & (z_ >= z))(lambda: copy(LEFT, slot).wait_send())
+
+
+def gather(own, owners, window_devs):
+    count = owners * window_devs
+    wide = 2 if window_devs == 1 else 1
+    shape = (count // (2 * wide), wide, window_devs)
+    return pl.pallas_call(
+        functools.partial(gather_kernel, shape),
+        out_shape=jax.ShapeDtypeStruct((count,) + own.shape, own.dtype),
+        in_specs=[pl.BlockSpec(memory_space=pltpu.VMEM)],
+        out_specs=pl.BlockSpec(memory_space=pltpu.VMEM),
+        scratch_shapes=[
+            pltpu.SemaphoreType.DMA((4, count)),
+            pltpu.SemaphoreType.DMA((count,)),
+            pltpu.SemaphoreType.DMA,
+        ],
+        compiler_params=pltpu.CompilerParams(
+            collective_id=0, has_side_effects=True, vmem_limit_bytes=40 * 2**20
+        ),
+        name="gather",
+    )(own)
+
+
 def local(traces, valid, pair_list):
     owners = lax.axis_size("pairs")
     window_devs = lax.axis_size("win")
-    me = lax.axis_index("pairs")
     samples = traces.shape[-1]
     per_window = traces.shape[2]
     windows = per_window * window_devs
     blk_count = traces.shape[0] // SB
-    pair_count = pair_list.shape[0] // owners
-    pairs = pair_count // window_devs
-    capacity = max(1, 4 * pair_count // owners)
-    series = ROWS * per_window
-    masked = (traces * valid[:, None, :, None].astype(traces.dtype)).reshape(-1, samples)
-
-    requests = pair_list.reshape(owners, 2 * pair_count)
-    sources = requests // blk_count
-    ids = jnp.arange(2 * pair_count, dtype=jnp.int32)
-    earlier = ids[None, :] < ids[:, None]
-    ranks = jnp.sum((sources[:, :, None] == sources[:, None, :]) & earlier[None], axis=-1)
-    slots = jnp.arange(capacity, dtype=jnp.int32)
-    found = (sources == me)[:, None, :] & (ranks[:, None, :] == slots[None, :, None])
-    picked = jnp.sum(jnp.where(found, requests[:, None, :] % blk_count + 1, 0), axis=-1) - 1
-    picked = jnp.broadcast_to(picked[:, None], (owners, window_devs, capacity)).reshape(-1, 1)
-    serial = jnp.arange(series, dtype=jnp.int32)
-    from_rows = jnp.where(picked < 0, -1, picked * series + serial).reshape(-1, 1)
-    sending = from_rows == jnp.arange(masked.shape[0], dtype=jnp.int32)[None, :]
-    sent = jnp.dot(sending.astype(jnp.bfloat16), masked, preferred_element_type=jnp.bfloat16)
-    received = lax.all_to_all(
-        sent.reshape(owners * window_devs, capacity * series, samples),
-        ("pairs", "win"),
-        split_axis=0,
-        concat_axis=0,
-        tiled=True,
-    ).reshape(-1, samples)
-
-    def kept(array):
-        own = lax.dynamic_index_in_dim(array, me, 0, keepdims=False).reshape(pair_count, 2)
-        own = lax.dynamic_slice_in_dim(own, lax.axis_index("win") * pairs, pairs, 0)
-        return own.T[:, None, None, None, :]
-
-    i = jnp.arange(ROWS, dtype=jnp.int32)[None, :, None, None, None]
-    v = jnp.arange(window_devs, dtype=jnp.int32)[None, None, :, None, None]
-    w = jnp.arange(per_window, dtype=jnp.int32)[None, None, None, :, None]
-    slot = (kept(sources) * window_devs + v) * capacity + kept(ranks)
-    wanted = (slot * ROWS + i) * per_window + w
-    chosen = wanted.reshape(-1, 1) == jnp.arange(received.shape[0], dtype=jnp.int32)[None, :]
-    x = jnp.dot(chosen.astype(jnp.bfloat16), received, preferred_element_type=jnp.bfloat16)
+    pairs = pair_list.shape[0] // (owners * window_devs)
+    own_rows = blk_count * ROWS * per_window
+    masked = traces * valid[:, None, :, None].astype(traces.dtype)
+    everything = gather(masked.reshape(own_rows, samples), owners, window_devs)
+    everything = everything.reshape(-1, samples)
+    place = lax.axis_index("pairs") * window_devs + lax.axis_index("win")
+    mine = lax.dynamic_slice_in_dim(pair_list, place * pairs, pairs, 0).T
+    blocks = mine[:, None, None, None, :]
+    i = jnp.arange(ROWS)[None, :, None, None, None]
+    v = jnp.arange(window_devs)[None, None, :, None, None]
+    w = jnp.arange(per_window)[None, None, None, :, None]
+    device = blocks // blk_count * window_devs + v
+    wanted = device * own_rows + ((blocks % blk_count) * ROWS + i) * per_window + w
+    chosen = wanted.reshape(-1, 1) == jnp.arange(everything.shape[0])[None, :]
+    x = jnp.dot(chosen.astype(jnp.bfloat16), everything, preferred_element_type=jnp.bfloat16)
     return stack(x, pairs, windows)
 
 

time: 115 us -> 79.2 us (0.69)
  the two profiles are of different devices: /device:TPU:13 before, /device:TPU:0 now
where the time goes in v3:
time: 79.2 us; the launch traced here: 79.1 us
  Pallas kernels  72 us (91%)
  matrix products  3.82 us (5%)
  other arithmetic  2.87 us (4%)
    pallas_call x1, Pallas kernels, gather(): pl.pallas_call(functools.partial(gather_kernel, shape), out_shape=jax.Sha...  44 us
    pallas_call x1, Pallas kernels, stack(): pl.pallas_call(functools.partial(stack_kernel, pairs, windows), out_shape...  28 us
    dot_general x1, matrix products, local(): jnp.dot(chosen.astype(jnp.bfloat16), everything, preferred_element_type=j...  3.82 us

profile of v3, /device:TPU:0, one launch (start us, length us, event | category | flops | bytes accessed | tf_op | source)
XLA Modules:
  0.0 79.1 jit_solution(2503116179820692026)
XLA Ops:
  0.0 0.7 convert_element_type.5
  0.7 0.8 fusion.3
  1.4 0.1 copy.7
  1.6 0.1 add.76
  1.6 1.4 %broadcast_multiply_fusion = bf16[16,3,2,2048]{3,2,1,0:T(2,128)(2,1)S(1)} fusion(bf16[16,3,2,2048]{3,2,1,0:T(2,128)(2,1)} %param.6, bf16[16,2]{1,0:T(8,128)(2,1)S(1)} %copy.7), kind=kLoop, calls=%fused_computation.3 | loop fusion | flops 196608 | bytes 786496 | tf_op jit(solution)/shard_map/mul | solution.py:235
  3.1 0.1 reshape.71.own_ref
  3.2 44.0 %gather.1 = bf16[16,96,2048]{2,1,0:T(8,128)(2,1)S(1)} custom-call(bf16[96,2048]{1,0:T(8,128)(2,1)S(1)} %reshape.71.own_ref), custom_call_target="tpu_custom_call" | custom-call | tf_op jit(solution)/shard_map/gather/pallas_call | solution.py:209
  47.3 3.8 %fusion.x_ref = bf16[384,2048]{1,0:T(8,128)(2,1)} fusion(bf16[1536,2048]{1,0:T(8,128)(2,1)S(1)} %bitcast.27, s32[384]{0:T(512)S(1)} %add.76), kind=kOutput, calls=%fused_computation.1 | convolution fusion | flops 2416508928 | bytes 7865856 | tf_op jit(solution)/shard_map/dot_general | solution.py:247
  51.1 28.0 %stack.1 = f32[576,2048]{1,0:T(8,128)} custom-call(bf16[384,2048]{1,0:T(8,128)(2,1)} %fusion.x_ref, bf16[2,2048,2048]{2,1,0:T(8,128)(2,1)} %constant.51.clone.fwd_ref, bf16[256,256]{1,0:T(8,128)(2,1)} %constant.52.clone.band_ref, bf16[2,2048,2048]{2,1,0:T(8,128)(2,1)} %constant.53.clone.inv_ref), custom_call_target="tpu_custom_call" | custom-call | flops 16106127360 | bytes 38273024 | tf_op jit(solution)/shard_map/stack/pallas_call | solution.py:85
  (2 shorter events, 0.0 us)
